TPU v7x, 512 devices: a whole 4x8x8 slice. The times are simulated.
512 devices in a mesh: dp: 32 (over z, x), proto: 16 (over y, core).
Axes of the slice: x: 4, y: 8, z: 8, core: 2. Of those that a mesh axis runs over, the one named last changes fastest.
Arguments:
- teacher: bfloat16 [4096, 384], P('dp'), may hold values from -6 to 6
- student: bfloat16 [4096, 384], P('dp'), may hold values from -6 to 6
- proto_weight: bfloat16 [384, 131072], P('dp', 'proto'), may hold values from -0.6 to 0.6
- cotangent: float32 [4096], P('dp'), may hold values from 64 to 1024
Outputs:
- crop_loss: float32 [4096], P('dp')
- feature_grad: float32 [4096, 384], P('dp')
All inputs are finite; a program needn't handle non-finite values.
Results may differ from a plain program's by a relative error of at most 0.0028.
Values may be sent and summed in bfloat16 or wider, within the bound.
A program may use at most 64 MiB of HBM per device.

v0:
```python
import jax
import jax.numpy as jnp
from jax import lax
from jax.sharding import PartitionSpec as P

ITERS = 3


epsilon = 1e-06
teacher_temp = 0.04
student_temp = 0.1


def normalize_rows(values):
    values_f = values.astype(jnp.float32)
    inv_norm = lax.rsqrt(jnp.sum(values_f * values_f, axis=1, keepdims=True) + epsilon)
    return (values_f * inv_norm, inv_norm)


def column_step(teacher_exp, row_scale):
    partial_cols = jnp.sum(teacher_exp * row_scale, axis=0, keepdims=True)
    return 1.0 / lax.psum(partial_cols.astype(jnp.bfloat16), "dp").astype(jnp.float32)


def shards(teacher, student, proto_weight, cotangent):
    teacher_norm, unused_inv = normalize_rows(teacher)
    student_norm, inv_student = normalize_rows(student)
    batch = teacher.shape[0]
    features = jnp.concatenate([teacher_norm, student_norm], axis=0).astype(jnp.bfloat16)
    assembled = lax.all_gather(proto_weight, "dp", axis=0, tiled=True)
    scores = jnp.dot(features, assembled, preferred_element_type=jnp.float32)
    col_squares = jnp.sum(jnp.square(assembled.astype(jnp.float32)), axis=0, keepdims=True)
    inv_proto = lax.rsqrt(col_squares + epsilon)
    cosines = scores * inv_proto
    teacher_exp = jnp.exp(cosines[:batch] / teacher_temp)
    student_logit = cosines[batch:] / student_temp
    student_exp = jnp.exp(student_logit)
    local_total = jnp.sum(student_exp, axis=1, keepdims=True)
    row_scale = jnp.ones((batch, 1), jnp.float32)
    for sweep in range(ITERS):
        col_scale = column_step(teacher_exp, row_scale)
        partial_rows = jnp.sum(teacher_exp * col_scale, axis=1, keepdims=True)
        row_scale = 1.0 / lax.psum(partial_rows, "proto")
    target = teacher_exp * row_scale * col_scale
    local_cross = jnp.sum(target * student_logit, axis=1, keepdims=True)
    exp_total, cross_term = lax.psum((local_total, local_cross), "proto")
    crop_loss = (jnp.log(exp_total) - cross_term)[:, 0]
    soft = student_exp / exp_total
    dscaled = (cotangent[:, None] * (soft - target) / student_temp * inv_proto).astype(jnp.bfloat16)
    partial_grad = lax.dot_general(
        dscaled,
        lax.all_gather(proto_weight, "dp", axis=0, tiled=True),
        (((1,), (1,)), ((), ())),
        preferred_element_type=jnp.float32,
    )
    unit_grad = lax.psum(partial_grad, "proto")
    along = jnp.sum(student_norm * unit_grad, axis=1, keepdims=True)
    feature_grad = (unit_grad - student_norm * along) * inv_student
    return (crop_loss, feature_grad)


def solution(mesh):
    return jax.shard_map(
        shards,
        mesh=mesh,
        in_specs=(P("dp", None), P("dp", None), P("dp", "proto"), P("dp")),
        out_specs=(P("dp"), P("dp", None)),
        check_vma=False,
    )
```

profile of v0, /device:TPU:1, one launch (start us, length us, event | category | flops | bytes accessed | tf_op | source)
XLA Modules:
  0.0 796.8 jit_solution(3049276510185917284)
XLA Ops:
  7.2 0.0 all-gather.3.cloned.1.call-start
  7.2 0.7 all-gather.3.cloned.1.call-update
  7.9 0.0 all-reduce.3.cloned.1.call-start
  7.9 1.0 fusion.5
  8.9 1.0 fusion.10
  10.0 1.0 fusion.4
  11.0 109.8 %all-gather.3.cloned.1.call-done = bf16[32,12,8192]{2,1,0:T(8,128)(2,1)} async-done(((bf16[1,12,8192]{2,1,0:T(8,128)(2,1)}), bf16[32,12,8192]{2,1,0:T(8,128)(2,1)}) %all-gather.3.cloned.1.call-update) | async-done | bytes 6291472 | tf_op jit(solution)/shard_map/all_gather | solution.py:30
  120.8 8.7 %reshape.52 = bf16[384,8192]{1,0:T(8,128)(2,1)} reshape(bf16[32,12,8192]{2,1,0:T(8,128)(2,1)} %all-gather.3.cloned.1.call-done) | data formatting | bytes 12582912
  129.6 4.3 multiply_reduce_fusion
  133.9 0.3 copy-done.1
  134.2 2.4 convolution_multiply_fusion
  136.6 3.2 copy-done
  139.8 0.6 fusion.17
  140.4 111.8 %psum.64 = bf16[1,8192]{1,0:T(2,128)(2,1)S(1)} all-reduce(bf16[1,8192]{1,0:T(2,128)(2,1)S(1)} %convert_element_type.68), channel_id=1, replica_groups=mesh['dp'=32,'proto'=16] {'dp'}, use_global_device_ids=true, to_apply=%region_6.0 | all-reduce | flops 8192 | bytes 32768 | tf_op jit(solution)/shard_map/psum | solution.py:22
  252.3 4.9 exponential_reduce_fusion
  257.2 51.4 %psum.65 = f32[128,1]{0,1:T(1,128)S(1)} all-reduce(f32[128,1]{0,1:T(1,128)S(1)} %bitcast.28), channel_id=1, replica_groups=mesh['dp'=32,'proto'=16] {'proto'}, use_global_device_ids=true, to_apply=%region_8.0 | all-reduce | flops 128 | bytes 1024 | tf_op jit(solution)/shard_map/psum | solution.py:43
  308.6 3.0 multiply_reduce_fusion.5
  311.6 109.9 %psum.66 = bf16[1,8192]{1,0:T(2,128)(2,1)S(1)} all-reduce(bf16[1,8192]{1,0:T(2,128)(2,1)S(1)} %convert_element_type.71), channel_id=1, replica_groups=mesh['dp'=32,'proto'=16] {'dp'}, use_global_device_ids=true, to_apply=%region_10.0 | all-reduce | flops 8192 | bytes 32768 | tf_op jit(solution)/shard_map/psum | solution.py:22
  421.6 3.0 multiply_reduce_fusion.4
  424.5 51.3 %psum.67 = f32[128,1]{0,1:T(1,128)S(1)} all-reduce(f32[128,1]{0,1:T(1,128)S(1)} %bitcast.29), channel_id=1, replica_groups=mesh['dp'=32,'proto'=16] {'proto'}, use_global_device_ids=true, to_apply=%region_12.0 | all-reduce | flops 128 | bytes 1024 | tf_op jit(solution)/shard_map/psum | solution.py:43
  475.9 3.0 multiply_reduce_fusion.3
  478.8 109.9 %psum.68 = bf16[1,8192]{1,0:T(2,128)(2,1)S(1)} all-reduce(bf16[1,8192]{1,0:T(2,128)(2,1)S(1)} %convert_element_type.74), channel_id=1, replica_groups=mesh['dp'=32,'proto'=16] {'dp'}, use_global_device_ids=true, to_apply=%region_14.0 | all-reduce | flops 8192 | bytes 32768 | tf_op jit(solution)/shard_map/psum | solution.py:22
  588.8 2.9 multiply_reduce_fusion.2
  591.8 51.3 %psum.69 = f32[128,1]{0,1:T(1,128)S(1)} all-reduce(f32[128,1]{0,1:T(1,128)S(1)} %bitcast.30), channel_id=1, replica_groups=mesh['dp'=32,'proto'=16] {'proto'}, use_global_device_ids=true, to_apply=%region_16.0 | all-reduce | flops 128 | bytes 1024 | tf_op jit(solution)/shard_map/psum | solution.py:43
  643.1 4.7 multiply_reduce_fusion.1
  647.8 23.7 %all-reduce = (f32[128,1]{0,1:T(1,128)S(1)}, f32[128,1]{0,1:T(1,128)S(1)}) all-reduce(f32[128,1]{0,1:T(1,128)S(1)} %bitcast.27, f32[128,1]{0,1:T(1,128)S(1)} %bitcast.26), channel_id=1, replica_groups=mesh['dp'=32,'proto'=16] {'proto'}, use_global_device_ids=true, to_apply=%region_18.0 | all-reduce | flops 256 | bytes 2048 | tf_op jit(solution)/shard_map/psum | solution.py:46
  671.5 8.3 %fusion.1 = f32[128,384]{1,0:T(8,128)} fusion(bf16[384,8192]{1,0:T(8,128)(2,1)} %reshape.52, f32[256,8192]{1,0:T(8,128)} %copy-done, f32[8192]{0:T(1024)S(1)} %get-tuple-element.6, f32[128]{0:T(128)S(1)} %bitcast.31, f32[128]{0:T(128)S(1)} %copy-done.3, f32[128]{0:T(128)S(1)} %divide_bitcast_fusion, f32[8192]{0:T(1024)S(1)} %bitcast.22), kind=kOutput, calls=%fused_computation.14 | convolution fusion | flops 814743552 | bytes 14943744 | tf_op jit(solution)/shard_map/dot_general | solution.py:50
  679.9 0.0 all-reduce.3.cloned.1.call-update
  679.9 0.5 subtract_bitcast_fusion
  680.4 106.7 %all-reduce.3.cloned.1.call-done = f32[128,384]{1,0:T(8,128)} async-done(((f32[128,384]{1,0:T(8,128)}), f32[128,384]{1,0:T(8,128)}) %all-reduce.3.cloned.1.call-update) | async-done | bytes 196624 | tf_op jit(solution)/shard_map/psum | solution.py:56
  787.1 1.1 fusion.7
  788.2 1.7 fusion.9
  (18 shorter events, 0.2 us)
Async XLA Ops:
  7.2 113.7 %all-gather.3.cloned.1.call-start = ((), (), s32[]{:S(2)}) async-start(), calls=%async_computation.1 | async-start | bytes 8650752 | tf_op jit(solution)/shard_map/all_gather | solution.py:30
  7.9 779.2 %all-reduce.3.cloned.1.call-start = ((), (), s32[]{:S(2)}) async-start(), calls=%async_computation | async-start | bytes 393216 | tf_op jit(solution)/shard_map/psum | solution.py:56
  129.6 4.6 copy-start.1
  136.6 3.2 copy-start
  643.1 28.4 %copy-start.3 = (f32[128]{0:T(128)S(1)}, f32[128]{0:T(128)}, u32[]{:S(2)}) copy-start(f32[128]{0:T(128)} %param.7) | copy-start | bytes 1540
  671.5 115.6 %copy-start.2 = (bf16[128,384]{1,0:T(8,128)(2,1)S(1)}, bf16[128,384]{1,0:T(8,128)(2,1)}, u32[]{:S(2)}) copy-start(bf16[128,384]{1,0:T(8,128)(2,1)} %param.5) | copy-start | bytes 294916
Sparse Core Ops, SparseCore 0:
  11.2 109.6 all-gather.2
  680.0 107.0 all-reduce.2
where the time goes:
time: 797 us
  blocking collectives  509 us (64%)
  waiting for transfers between devices  217 us (27%)
  other arithmetic  32.8 us (4%)
  between operations  14.1 us (2%)
  local copies, waits for them, and re-layouts  12.3 us (2%)
  matrix products  10.7 us (1%)
    psum x3, blocking collectives, column_step(): lax.psum(partial_cols.astype(jnp.bfloat16), 'dp').astype(jnp.float32)  332 us
    psum x3, blocking collectives, shards(): row_scale = 1.0 / lax.psum(partial_rows, 'proto')  154 us
    all_gather x1, waiting for transfers between devices, shards(): assembled = lax.all_gather(proto_weight, 'dp', axis=0, tiled=True)  110 us
    psum x1, waiting for transfers between devices, shards(): unit_grad = lax.psum(partial_grad, 'proto')  107 us
    psum x1, blocking collectives, shards(): exp_total, cross_term = lax.psum((local_total, local_cross), 'proto')  23.7 us
  transfers between devices with their start and end apart: 2, of which 2 were waited for; matrix products, arithmetic and copies ran while one was open for 0% of the time, Pallas kernels for 0%

commit v1 on v0

v1 whole, which is shorter than its diff:
```python
import math

import jax
import jax.numpy as jnp
from jax import lax
from jax.experimental import pallas as pl
from jax.experimental.pallas import tpu as pltpu
from jax.sharding import PartitionSpec as P

EPS = 1e-06
LOG2E = math.log2(math.e)
T_SCALE = LOG2E / 0.04
S_SCALE = LOG2E / 0.1
F32, BF16 = jnp.float32, jnp.bfloat16
MESH = pl.DeviceIdType.MESH
HIGHEST = lax.Precision.HIGHEST
NT = (((1,), (1,)), ((), ()))

FAR_FIRST = (4, 3, 5, 2, 6, 1, 7)

T_Z, W_Z, S_Z = 0, 1, 3
RING = 4
COLS = 20
ROW_Y, ROW_Z = 23, 26
G1_A, G1_B, G2_A, G2_B, U_A, U_B, FIN, FIN_CORE = range(29, 37)
T_Y, S_Y = 37, 41
COUNT = 45


def unit_rows(values):
    inv = lax.rsqrt(jnp.sum(values * values, axis=1, keepdims=True) + EPS)
    return values * inv, inv


def fold(terms):
    while len(terms) > 1:
        terms = [a + b for a, b in zip(terms[::2], terms[1::2])]
    return terms[0]


def kernel(
    t_hbm, s_hbm, w_hbm, cot_hbm,
    grad_ref, loss_ref,
    t_ref, s_ref, w_ref, cot_ref, perm_ref,
    pack, wz_send, wz_buf, wz_wide, asm, wb,
    fz_send, fz_buf, ft, sz_send, sz_buf, fs,
    e_ref, l_ref, pb, rowacc, rowacc2, eacc, rb, xb, ivec, cvec,
    c_send, c_buf, ry_send, ry_buf, rz_send, rz_buf,
    ga, gb, g1a_send, g1a_buf, g1b_send, g1b_buf, g2a_send, g2a_buf, g2b_send, g2b_buf,
    ua_send, ua_buf, ub_send, ub_buf, csum, vec, lry_send, lry_buf, lrz_send, lrz_buf,
    col_cot, col_x, own_unit,
    fin_send, fin_buf,
    lsem, ssem, rsem,
):
    dp, pr = lax.axis_index("dp"), lax.axis_index("proto")
    z, x = lax.div(dp, 4), lax.rem(dp, 4)
    y, k = lax.div(pr, 2), lax.rem(pr, 2)

    def z_peer(i):
        return (lax.rem(z + i, 8) * 4 + x, pr)

    def y_peer(i):
        return (dp, lax.rem(y + i, 8) * 2 + k)

    def xk_peer(i):
        g = lax.rem(x * 2 + k + i, 8)
        return (z * 4 + lax.div(g, 2), y * 2 + lax.rem(g, 2))

    def a_peer(i):
        y_at, z_at = y_peer(i)[1], z_peer(i)[0]
        return (dp + k * (z_at - dp), y_at + k * (pr - y_at))

    def b_peer(i):
        y_at, z_at = y_peer(i)[1], z_peer(i)[0]
        return (z_at + k * (dp - z_at), pr + k * (y_at - pr))

    a_me, b_me = y + k * (z - y), z + k * (y - z)
    a_step, b_step = 64 - 56 * k, 8 + 56 * k

    def crops(a, b):
        return pl.ds(pl.multiple_of(a * a_step + b * b_step, 8), 8)

    def copy(src, dst, sem, peer):
        return pltpu.make_async_remote_copy(
            src_ref=src, dst_ref=dst, send_sem=ssem.at[sem], recv_sem=rsem.at[sem],
            device_id=peer, device_id_type=MESH,
        )

    def got(ref, sem):
        copy(ref, ref, sem, (dp, pr)).wait_recv()

    def sent(ref, sem):
        copy(ref, ref, sem, (dp, pr)).wait_send()

    half = lax.rem(y, 2)
    at16 = pl.multiple_of(k * 64 + lax.div(y, 2) * 16, 16)
    rows16 = pl.ds(at16, 16)
    loads = [
        pltpu.make_async_copy(src, dst, lsem.at[n])
        for n, (src, dst) in enumerate((
            (t_hbm.at[rows16], t_ref), (w_hbm, w_ref), (s_hbm.at[rows16], s_ref), (cot_hbm, cot_ref)
        ))
    ]
    for load in loads:
        load.start()

    barrier = pltpu.get_barrier_semaphore()
    for i in range(1, 8):
        for peer in (z_peer(i), y_peer(i), xk_peer(i)):
            pl.semaphore_signal(barrier, inc=1, device_id=peer, device_id_type=MESH)

    feature = lax.broadcasted_iota(jnp.int32, (384, 128), 0)
    fz = lax.shift_right_logical(feature * 1366, 16)
    fx = lax.shift_right_logical((feature - fz * 48) * 5462, 16)
    place = fx * 96 + fz * 12 + (feature - fz * 48 - fx * 12)
    lane = lax.broadcasted_iota(jnp.int32, (384, 128), 1)
    for n in range(3):
        perm_ref[:, 128 * n:128 * n + 128] = (place == lane + 128 * n).astype(F32).astype(BF16)

    def own_rows(ref, send, buf):
        v = unit_rows(ref[...].astype(F32))[0].astype(BF16)
        v = jnp.dot(v, perm_ref[...], preferred_element_type=F32)
        v = jnp.where(half == 0, v[0:8], v[8:16])
        send[...] = v
        buf[z] = v

    loads[0].wait()
    own_rows(t_ref, fz_send, fz_buf)
    loads[1].wait()
    for d in range(8):
        for h in range(2):
            for r in range(4):
                q, at = d * 8 + h * 4 + r, ((h * 8 + d) * 4 + r) * 12
                pack[at:at + 12, :] = w_ref[:, 128 * q:128 * q + 128].astype(F32)
    for h in range(2):
        for d in range(8):
            at = (h * 8 + d) * 48
            wz_send[h, d] = pack[at:at + 48, :].astype(BF16)
        wz_buf[h, z] = wz_send[h, z]

    pl.semaphore_wait(barrier, 21)

    for i in FAR_FIRST:
        copy(fz_send, fz_buf.at[z], T_Z, z_peer(i)).start()
    for h in range(2):
        for i in FAR_FIRST:
            copy(wz_send.at[h, lax.rem(z + i, 8)], wz_buf.at[h, z], W_Z + h, z_peer(i)).start()

    loads[2].wait()
    own_rows(s_ref, sz_send, sz_buf)
    for i in FAR_FIRST:
        copy(sz_send, sz_buf.at[z], S_Z, z_peer(i)).start()

    first, second = pl.ds(0, 32), pl.ds(32, 32)

    def rows_out(buf, at):
        block = buf.at[y]
        copy(block, block, at + 1, y_peer(2)).start()
        copy(block, block, at + 2, y_peer(6)).start()
        copy(block, block, at, y_peer(1)).start()
        copy(block, block, at, y_peer(7)).start()

    def rows_on(buf, at):
        below, above = buf.at[lax.rem(y + 6, 8)], buf.at[lax.rem(y + 2, 8)]
        got(below, at + 1)
        copy(below.at[first], below.at[first], at + 3, y_peer(2)).start()
        copy(below, below, at + 3, y_peer(1)).start()
        got(above, at + 2)
        copy(above.at[second], above.at[second], at + 3, y_peer(6)).start()
        copy(above, above, at + 3, y_peer(7)).start()

    def rows_in(buf, at):
        got(buf.at[pl.ds(0, 2)], at)
        got(buf.at[pl.ds(0, 3)], at + 3)

    got(fz_buf.at[pl.ds(0, 7)], T_Z)
    ft[y] = fz_buf[...].reshape(64, 384).astype(BF16)
    rows_out(ft, T_Y)

    x_right, x_left, x_far = lax.rem(x + 1, 4), lax.rem(x + 3, 4), lax.rem(x + 2, 4)
    right, left, core = (z * 4 + x_right, pr), (z * 4 + x_left, pr), (dp, y * 2 + 1 - k)
    low, high = pl.ds(0, 48), pl.ds(48, 48)

    def piece(h, at):
        return wb.at[h, k, at]

    for h in range(2):
        got(wz_buf.at[h, pl.ds(0, 7)], W_Z + h)
        for s in range(8):
            wz_wide[s] = wz_buf[h, s].astype(F32)
            for q in range(4):
                asm[12 * s:12 * s + 12, 128 * q:128 * q + 128] = wz_wide[s, 12 * q:12 * q + 12, :]
        wb[h, k, x] = asm[...].astype(BF16)
        own = piece(h, x)
        copy(own, own, RING + 8 * h, right).start()
        copy(own, own, RING + 8 * h + 1, left).start()
        copy(own, own, RING + 8 * h + 4, core).start()
        if h == 0:
            rows_on(ft, T_Y)
    got(sz_buf.at[pl.ds(0, 7)], S_Z)
    fs[y] = sz_buf[...].reshape(64, 384).astype(BF16)
    rows_out(fs, S_Y)
    for h in range(2):
        at, from_left, from_right = RING + 8 * h, piece(h, x_left), piece(h, x_right)
        got(from_left, at)
        copy(from_left.at[low], from_left.at[low], at + 2, right).start()
        got(from_right, at + 1)
        copy(from_right.at[high], from_right.at[high], at + 3, left).start()
        copy(from_left, from_left, at + 5, core).start()
        copy(from_right, from_right, at + 6, core).start()

    def far_piece(h):
        far = piece(h, x_far)
        got(far.at[low], RING + 8 * h + 2)
        got(far.at[high], RING + 8 * h + 3)
        copy(far, far, RING + 8 * h + 7, core).start()

    far_piece(0)
    rows_in(ft, T_Y)
    far_piece(1)

    def chunk(q):
        h, kk, c0 = lax.div(q, 4), lax.rem(lax.div(q, 2), 2), pl.multiple_of(lax.rem(q, 2) * 256, 256)
        return wb[h, kk, :, :, pl.ds(c0, 256)].reshape(384, 256), pl.ds(pl.multiple_of(q * 256, 256), 256)

    def teacher_chunk(q, carry):
        w, at = chunk(q)
        wf = w.astype(F32)
        inv = lax.rsqrt(jnp.sum(wf * wf, axis=0, keepdims=True) + EPS)
        scores = jnp.dot(ft[...].reshape(512, 384), w, preferred_element_type=F32)
        e = jnp.exp2(scores * (inv * T_SCALE))
        e_ref[:, at] = e
        col = jnp.sum(e, axis=0, keepdims=True)
        for n in range(2):
            part = slice(128 * n, 128 * n + 128)
            ivec[pl.ds(2 * q + n, 1), :] = inv[:, part]
            csum[pl.ds(2 * q + n, 1), :] = col[:, part]
        return carry

    for h in range(2):
        for n in range(4):
            got(piece(h, x), RING + 8 * h + 4 + n)
        lax.fori_loop(4 * h, 4 * h + 4, teacher_chunk, 0)
        if h == 0:
            rows_on(fs, S_Y)

    def columns_start(it):
        c_send[it] = csum[...].astype(BF16)
        for i in FAR_FIRST:
            copy(c_send.at[it], c_buf.at[it, i - 1], COLS + it, xk_peer(i)).start()

    def columns_end(it):
        got(c_buf.at[it], COLS + it)
        cvec[...] = 1.0 / fold([c_send[it].astype(F32)] + [c_buf[it, i].astype(F32) for i in range(7)])

    def row_pass():
        scale = [cvec[q:q + 1, :] for q in range(16)]

        def body(i, carry):
            rows = pl.ds(pl.multiple_of(i * 16, 16), 16)
            rowacc[rows, :] = fold([e_ref[rows, 128 * q:128 * q + 128] * scale[q] for q in range(16)])
            return carry

        lax.fori_loop(0, 32, body, 0, unroll=4)

    def lanes(ref):
        return [jnp.sum(jnp.transpose(ref[128 * j:128 * j + 128, :]), axis=0, keepdims=True) for j in range(4)]

    def put(dst, at, sums):
        for j in range(4):
            dst[at + j:at + j + 1, :] = sums[j]

    def row_refs(it):
        if it == 2:
            return lry_send, lry_buf, lrz_send, lrz_buf
        return ry_send.at[it], ry_buf.at[it], rz_send.at[it], rz_buf.at[it]

    def added(own, buf):
        return fold([own[...]] + [buf[i] for i in range(7)])

    def rows_start(it):
        y_send, y_buf, _, _ = row_refs(it)
        put(y_send, 0, lanes(rowacc))
        for i in FAR_FIRST:
            copy(y_send, y_buf.at[i - 1], ROW_Y + it, y_peer(i)).start()

    def rows_middle(it):
        y_send, y_buf, z_send, z_buf = row_refs(it)
        got(y_buf, ROW_Y + it)
        z_send[...] = added(y_send, y_buf)
        for i in FAR_FIRST:
            copy(z_send, z_buf.at[i - 1], ROW_Z + it, z_peer(i)).start()

    def turn(row):
        return jnp.transpose(jnp.broadcast_to(row, (128, 128)))

    def rows_end(it):
        _, _, z_send, z_buf = row_refs(it)
        got(z_buf, ROW_Z + it)
        total = added(z_send, z_buf)
        r = 1.0 / total[0:4, :]
        for j in range(4):
            rb[128 * j:128 * j + 128, :] = turn(r[j:j + 1, :])
        return total

    def column_pass():
        def body(i, acc):
            rows = pl.ds(pl.multiple_of(i * 8, 8), 8)
            r8 = rb[rows, :]
            return tuple(acc[q] + e_ref[rows, 128 * q:128 * q + 128] * r8 for q in range(16))

        acc = lax.fori_loop(0, 64, body, tuple(jnp.zeros((8, 128), F32) for _ in range(16)), unroll=4)
        for q in range(16):
            csum[q:q + 1, :] = jnp.sum(acc[q], axis=0, keepdims=True)

    def student_chunk(q, carry):
        w, at = chunk(q)
        inv = jnp.concatenate([ivec[pl.ds(2 * q, 1), :], ivec[pl.ds(2 * q + 1, 1), :]], axis=1)
        logits = jnp.dot(fs[...].reshape(512, 384), w, preferred_element_type=F32) * (inv * S_SCALE)
        l_ref[:, at] = logits
        p = jnp.exp2(logits)
        eacc[...] += p[:, :128] + p[:, 128:]
        pb[:, at] = (p * inv).astype(BF16)
        return carry

    def product(first, last):
        total = None
        for n in range(4):
            h, kk = divmod(n, 2)
            term = lax.dot_general(
                pb[:, 512 * n:512 * n + 512], wb[h, kk].reshape(384, 512)[first:last], NT, preferred_element_type=F32
            )
            total = term if total is None else total + term
        return total

    def gradient_a(dst):
        ga[...] = product(0, 256)
        for a in range(8):
            dst[a] = jnp.concatenate([ga[crops(a, b), :] for b in range(8)], axis=0).astype(BF16)

    def gradient_b(dst):
        gb[...] = product(256, 384)
        for b in range(8):
            dst[b] = jnp.concatenate([gb[crops(a, b), :] for a in range(8)], axis=0).astype(BF16)

    def spread_a(src, dst, sem):
        for i in FAR_FIRST:
            copy(src.at[lax.rem(a_me + i, 8)], dst.at[i - 1], sem, a_peer(i)).start()

    def spread_b(src, dst, sem):
        for i in FAR_FIRST:
            copy(src.at[lax.rem(b_me + i, 8)], dst.at[i - 1], sem, b_peer(i)).start()

    columns_start(0)
    lry_send[...] = jnp.zeros_like(lry_send)
    eacc[...] = jnp.zeros_like(eacc)
    loads[3].wait()
    col_cot[...] = turn(cot_ref[...])
    columns_end(0)
    row_pass()
    rows_start(0)
    rows_in(fs, S_Y)
    lax.fori_loop(0, 2, student_chunk, 0)
    rows_middle(0)
    lax.fori_loop(2, 5, student_chunk, 0)
    rows_end(0)
    column_pass()
    columns_start(1)
    lax.fori_loop(5, 8, student_chunk, 0)
    columns_end(1)
    row_pass()
    rows_start(1)
    gradient_a(g1a_send)
    rows_middle(1)
    spread_a(g1a_send, g1a_buf, G1_A)
    gradient_b(g1b_send)
    rows_end(1)
    spread_b(g1b_send, g1b_buf, G1_B)
    column_pass()
    columns_start(2)
    s16 = unit_rows(s_ref[...].astype(F32))
    s8, inv8 = (jnp.where(half == 0, v[0:8], v[8:16]) for v in s16)
    put(lry_send, 8, lanes(eacc))
    own_unit[...] = jnp.dot(s8, perm_ref[...].astype(F32), precision=HIGHEST, preferred_element_type=F32)
    columns_end(2)

    c_rows = [cvec[q:q + 1, :] for q in range(16)]
    i_rows = [ivec[q:q + 1, :] for q in range(16)]

    def last_pass(i, carry):
        rows = pl.ds(pl.multiple_of(i * 16, 16), 16)
        acc, acc2 = [], []
        for q in range(16):
            at = slice(128 * q, 128 * q + 128)
            v = e_ref[rows, at] * c_rows[q]
            acc.append(v)
            acc2.append(v * l_ref[rows, at])
            pb[rows, at] = (v * i_rows[q]).astype(BF16)
        rowacc[rows, :] = fold(acc)
        rowacc2[rows, :] = fold(acc2)
        return carry

    lax.fori_loop(0, 32, last_pass, 0, unroll=2)
    put(lry_send, 4, lanes(rowacc2))
    rows_start(2)
    gradient_a(g2a_send)
    spread_a(g2a_send, g2a_buf, G2_A)
    gradient_b(g2b_send)
    rows_middle(2)
    spread_b(g2b_send, g2b_buf, G2_B)

    def sum_blocks(own, buf):
        return fold([own.astype(F32)] + [buf[i].astype(F32) for i in range(7)])

    def wide(block, times):
        return jnp.concatenate([block] * times, axis=1)

    got(g1a_buf, G1_A)
    got(g1b_buf, G1_B)
    g1a = sum_blocks(g1a_send[a_me], g1a_buf)
    g1b = sum_blocks(g1b_send[b_me], g1b_buf)
    total = rows_end(2)
    vec[...] = total
    inv_total = 1.0 / total[8:12, :]
    for j in range(4):
        xb[128 * j:128 * j + 128, :] = turn(inv_total[j:j + 1, :])
    col_x[...] = turn(vec[pl.ds(lax.div(y, 2) + 4, 1), :])
    got(g2b_buf, G2_B)
    g2b = sum_blocks(g2b_send[b_me], g2b_buf)
    for a in range(8):
        rows, part = crops(a, b_me), slice(8 * a, 8 * a + 8)
        ub_send[a] = g1b[part] * xb[rows, :] - g2b[part] * rb[rows, :]
    for i in FAR_FIRST:
        copy(ub_send.at[lax.rem(a_me + i, 8)], ub_buf.at[i - 1], U_B, a_peer(i)).start()
    got(g2a_buf, G2_A)
    g2a = sum_blocks(g2a_send[a_me], g2a_buf)
    for b in range(8):
        rows, part = crops(a_me, b), slice(8 * b, 8 * b + 8)
        ua_send[b] = g1a[part] * wide(xb[rows, :], 2) - g2a[part] * wide(rb[rows, :], 2)
    for i in FAR_FIRST:
        copy(ua_send.at[lax.rem(b_me + i, 8)], ua_buf.at[i - 1], U_A, b_peer(i)).start()

    rows8 = pl.ds(pl.multiple_of(y * 64 + z * 8, 8), 8)
    cross = rb[rows8, :] * col_x[pl.ds(pl.multiple_of(half * 64 + z * 8, 8), 8), :]
    loss8 = -jnp.log(xb[rows8, :]) - math.log(2.0) * cross
    cot8 = wide(col_cot[pl.ds(pl.multiple_of(k * 64 + y * 8, 8), 8), :], 3)
    got(ub_buf, U_B)
    u_b = added(ub_send.at[a_me], ub_buf)
    got(ua_buf, U_A)
    u8 = jnp.concatenate([added(ua_send.at[b_me], ua_buf), u_b], axis=1) * (cot8 / 0.1)
    unit8 = own_unit[...]
    along = jnp.sum(unit8 * u8, axis=1, keepdims=True)
    result = ((u8 - unit8 * along) * inv8).astype(BF16)
    result = lax.dot_general(result, perm_ref[...], NT, preferred_element_type=F32)
    first = loss8.astype(BF16).astype(F32)
    loss8 = jnp.where(lax.broadcasted_iota(jnp.int32, (8, 128), 1) < 64, first, loss8 - first)
    low_rows, high_rows = result[:, :256], jnp.concatenate([result[:, 256:], loss8], axis=1)
    result = jnp.concatenate([low_rows, high_rows], axis=0).astype(BF16)
    fin_send[...] = result
    fin_buf[k, y] = result
    for i in FAR_FIRST:
        copy(fin_send, fin_buf.at[k, y], FIN, y_peer(i)).start()
    got(fin_buf.at[k, pl.ds(0, 7)], FIN)
    copy(fin_buf.at[k], fin_buf.at[k], FIN_CORE, core).start()
    got(fin_buf.at[1 - k], FIN_CORE)
    out = fin_buf[...].reshape(16, 16, 256).astype(F32)
    grad_ref[:, :256] = out[:, :8, :].reshape(128, 256)
    grad_ref[:, 256:] = out[:, 8:, :128].reshape(128, 128)
    losses = jnp.transpose(out[:, 8:, 128:].reshape(128, 128))
    loss_ref[...] = losses[0:1, :] + losses[64:65, :]

    sent(fz_buf.at[pl.ds(0, 7)], T_Z)
    sent(sz_buf.at[pl.ds(0, 7)], S_Z)
    for buf, at in ((ft, T_Y), (fs, S_Y)):
        sent(buf.at[pl.ds(0, 2)], at)
        sent(buf.at[y], at + 1)
        sent(buf.at[y], at + 2)
        sent(buf.at[pl.ds(0, 3)], at + 3)
    for h in range(2):
        at, own = RING + 8 * h, piece(h, x)
        sent(wz_buf.at[h, pl.ds(0, 7)], W_Z + h)
        sent(own, at)
        sent(own, at + 1)
        sent(own.at[low], at + 2)
        sent(own.at[low], at + 3)
        for n in range(4):
            sent(own, at + 4 + n)
    for it in range(3):
        sent(c_buf.at[it], COLS + it)
        _, y_buf, _, z_buf = row_refs(it)
        sent(y_buf, ROW_Y + it)
        sent(z_buf, ROW_Z + it)
    for buf, sem in (
        (g1a_buf, G1_A), (g1b_buf, G1_B), (g2a_buf, G2_A), (g2b_buf, G2_B), (ua_buf, U_A), (ub_buf, U_B),
        (fin_buf.at[k, pl.ds(0, 7)], FIN), (fin_buf.at[k], FIN_CORE),
    ):
        sent(buf, sem)


def shards(teacher, student, proto_weight, cotangent):
    vmem, hbm = pl.BlockSpec(memory_space=pltpu.VMEM), pl.BlockSpec(memory_space=pltpu.HBM)
    v = pltpu.VMEM
    operands = (teacher, student, proto_weight, cotangent.reshape(1, 128))
    grad, loss = pl.pallas_call(
        kernel,
        out_shape=(v((128, 384), F32), v((1, 128), F32)),
        in_specs=[hbm] * 4,
        out_specs=(vmem, vmem),
        scratch_shapes=[
            v((16, 384), BF16), v((16, 384), BF16), v((12, 8192), BF16), v((1, 128), F32), v((384, 384), BF16),
            v((768, 128), F32), v((2, 8, 48, 128), BF16), v((2, 8, 48, 128), BF16), v((8, 48, 128), F32),
            v((96, 512), F32), v((2, 2, 4, 96, 512), BF16),
            v((8, 384), F32), v((8, 8, 384), F32), v((8, 64, 384), BF16),
            v((8, 384), F32), v((8, 8, 384), F32), v((8, 64, 384), BF16),
            v((512, 2048), F32), v((512, 2048), F32), v((512, 2048), BF16),
            v((512, 128), F32), v((512, 128), F32), v((512, 128), F32), v((512, 128), F32), v((512, 128), F32),
            v((16, 128), F32), v((16, 128), F32),
            v((3, 16, 128), BF16), v((3, 7, 16, 128), BF16),
            v((2, 4, 128), F32), v((2, 7, 4, 128), F32), v((2, 4, 128), F32), v((2, 7, 4, 128), F32),
            v((512, 256), F32), v((512, 128), F32),
            v((8, 64, 256), BF16), v((7, 64, 256), BF16), v((8, 64, 128), BF16), v((7, 64, 128), BF16),
            v((8, 64, 256), BF16), v((7, 64, 256), BF16), v((8, 64, 128), BF16), v((7, 64, 128), BF16),
            v((8, 8, 256), F32), v((7, 8, 256), F32), v((8, 8, 128), F32), v((7, 8, 128), F32),
            v((16, 128), F32), v((16, 128), F32), v((16, 128), F32), v((7, 16, 128), F32), v((16, 128), F32), v((7, 16, 128), F32),
            v((128, 128), F32), v((128, 128), F32), v((8, 384), F32),
            v((16, 256), BF16), v((2, 8, 16, 256), BF16),
            pltpu.SemaphoreType.DMA((4,)), pltpu.SemaphoreType.DMA((COUNT,)), pltpu.SemaphoreType.DMA((COUNT,)),
        ],
        compiler_params=pltpu.CompilerParams(
            collective_id=0, has_side_effects=True, vmem_limit_bytes=60 * 1024 * 1024
        ),
        cost_estimate=pl.CostEstimate(flops=2_400_000_000, bytes_accessed=4_000_000, transcendentals=2_000_000),
    )(*(pltpu.with_memory_space_constraint(a, pltpu.HBM) for a in operands))
    return loss.reshape(128), grad


def solution(mesh):
    return jax.shard_map(
        shards,
        mesh=mesh,
        in_specs=(P("dp", None), P("dp", None), P("dp", "proto"), P("dp")),
        out_specs=(P("dp"), P("dp", None)),
        check_vma=False,
    )
```

time: 797 us -> 93.6 us (0.12)
  blocking collectives: 509 us -> 0 us
  waiting for transfers between devices: 217 us -> 0 us
  Pallas kernels: 0 us -> 91.6 us
  other arithmetic: 32.8 us -> 0 us
  between operations: 14.1 us -> 0.64 us
  local copies, waits for them, and re-layouts: 12.3 us -> 1.19 us
  matrix products: 10.7 us -> 0 us
    psum x7 -> x0, blocking collectives: 509 us -> none  [the longest x3 332 us: column_step(): lax.psum(partial_cols.astype(jnp.bfloat16), 'dp').astype(jnp.float32)]
    all_gather x1 -> x0, waiting for transfers between devices: 110 us -> none  [shards(): assembled = lax.all_gather(proto_weight, 'dp', axis=0, tiled=True)]
    psum x1 -> x0, waiting for transfers between devices: 107 us -> none  [shards(): unit_grad = lax.psum(partial_grad, 'proto')]
    pallas_call x0 -> x1, Pallas kernels: none -> 91.6 us  [shards(): pl.pallas_call(kernel, out_shape=(v((128, 384), F32), v((1, 128), F32)),...]
    reduce_sum x11 -> x0, other arithmetic: 29.4 us -> none  [the longest x3 6.52 us: column_step(): partial_cols = jnp.sum(teacher_exp * row_scale, axis=0, keepdims=True)]
    unnamed x9 -> x2, local copies, waits for them, and re-layouts: 12.3 us -> 1.19 us
    dot_general x2 -> x0, matrix products: 10.7 us -> none  [the longest x1 8.35 us: shards(): lax.dot_general(dscaled, lax.all_gather(proto_weight, 'dp', axis=0, tiled...]
  transfers between devices with their start and end apart: 2 -> 0, of which waited for: 2 -> 0; matrix products, arithmetic and copies ran while one was open for 0% -> 0% of each run, Pallas kernels for 0% -> 0%
where the time goes in v1:
time: 93.6 us; the launch traced here: 93.5 us
  Pallas kernels  91.6 us (98%)
  local copies, waits for them, and re-layouts  1.19 us (1%)
    pallas_call x1, Pallas kernels, shards(): pl.pallas_call(kernel, out_shape=(v((128, 384), F32), v((1, 128), F32)),...  91.6 us

profile of v1, /device:TPU:1, one launch (start us, length us, event | category | flops | bytes accessed | tf_op | source)
XLA Modules:
  0.0 93.5 jit_solution(2841963914597747175)
XLA Ops:
  0.6 91.6 %shard_map.59 = (f32[128,384]{1,0:T(8,128)S(1)}, f32[1,128]{1,0:T(1,128)S(1)}) custom-call(bf16[128,384]{1,0:T(8,128)(2,1)} %t_hbm.1, bf16[128,384]{1,0:T(8,128)(2,1)} %s_hbm.1, bf16[12,8192]{1,0:T(8,128)(2,1)} %w_hbm.1, f32[1,128]{1,0:T(1,128)} %bitcast.3), custom_call_target="tpu_custom_call" | custom-call | flops 2400000000 | bytes 4000000 | tf_op jit(solution)/shard_map/pallas_call | solution.py:504
  92.3 0.5 copy.8
  92.8 0.7 copy.9

commit v2 on v1

--- a/solution.py
+++ b/solution.py
@@ -18,13 +18,13 @@
 
 FAR_FIRST = (4, 3, 5, 2, 6, 1, 7)
 
-T_Z, W_Z, S_Z = 0, 1, 3
+F_Z, W_Z = 0, 1
 RING = 4
-COLS = 20
-ROW_Y, ROW_Z = 23, 26
-G1_A, G1_B, G2_A, G2_B, U_A, U_B, FIN, FIN_CORE = range(29, 37)
-T_Y, S_Y = 37, 41
-COUNT = 45
+COLS = 24
+ROW_Y, ROW_Z = 27, 30
+G1_A, G1_B, G2_A, G2_B, U_A, U_B, FIN, FIN_CORE = range(33, 41)
+T_Y, S_Y = 41, 45
+COUNT = 49
 
 
 def unit_rows(values):
@@ -43,7 +43,7 @@
     grad_ref, loss_ref,
     t_ref, s_ref, w_ref, cot_ref, perm_ref,
     pack, wz_send, wz_buf, wz_wide, asm, wb,
-    fz_send, fz_buf, ft, sz_send, sz_buf, fs,
+    fz_send, fz_buf, ft, fs,
     e_ref, l_ref, pb, rowacc, rowacc2, eacc, rb, xb, ivec, cvec,
     c_send, c_buf, ry_send, ry_buf, rz_send, rz_buf,
     ga, gb, g1a_send, g1a_buf, g1b_send, g1b_buf, g2a_send, g2a_buf, g2b_send, g2b_buf,
@@ -117,15 +117,14 @@
     for n in range(3):
         perm_ref[:, 128 * n:128 * n + 128] = (place == lane + 128 * n).astype(F32).astype(BF16)
 
-    def own_rows(ref, send, buf):
-        v = unit_rows(ref[...].astype(F32))[0].astype(BF16)
-        v = jnp.dot(v, perm_ref[...], preferred_element_type=F32)
-        v = jnp.where(half == 0, v[0:8], v[8:16])
-        send[...] = v
-        buf[z] = v
-
     loads[0].wait()
-    own_rows(t_ref, fz_send, fz_buf)
+    loads[2].wait()
+    v = jnp.concatenate([t_ref[...].astype(F32), s_ref[...].astype(F32)], axis=0)
+    v = jnp.dot(unit_rows(v)[0].astype(BF16), perm_ref[...], preferred_element_type=F32)
+    v = [jnp.where(half == 0, v[at:at + 8], v[at + 8:at + 16]) for at in (0, 16)]
+    v = jnp.concatenate([m[:, 128 * n:128 * n + 128] for m in v for n in range(3)], axis=0).astype(BF16)
+    fz_send[...] = v
+    fz_buf[z] = v
     loads[1].wait()
     for d in range(8):
         for h in range(2):
@@ -141,15 +140,10 @@
     pl.semaphore_wait(barrier, 21)
 
     for i in FAR_FIRST:
-        copy(fz_send, fz_buf.at[z], T_Z, z_peer(i)).start()
+        copy(fz_send, fz_buf.at[z], F_Z, z_peer(i)).start()
     for h in range(2):
         for i in FAR_FIRST:
             copy(wz_send.at[h, lax.rem(z + i, 8)], wz_buf.at[h, z], W_Z + h, z_peer(i)).start()
-
-    loads[2].wait()
-    own_rows(s_ref, sz_send, sz_buf)
-    for i in FAR_FIRST:
-        copy(sz_send, sz_buf.at[z], S_Z, z_peer(i)).start()
 
     first, second = pl.ds(0, 32), pl.ds(32, 32)
 
@@ -173,8 +167,11 @@
         got(buf.at[pl.ds(0, 2)], at)
         got(buf.at[pl.ds(0, 3)], at + 3)
 
-    got(fz_buf.at[pl.ds(0, 7)], T_Z)
-    ft[y] = fz_buf[...].reshape(64, 384).astype(BF16)
+    got(fz_buf.at[pl.ds(0, 7)], F_Z)
+    for buf, at in ((ft, 0), (fs, 24)):
+        v = [fz_buf[d, :, :].astype(F32) for d in range(8)]
+        v = [jnp.concatenate([m[at + 8 * n:at + 8 * n + 8] for m in v], axis=0) for n in range(3)]
+        buf[y] = jnp.concatenate(v, axis=1).astype(BF16)
     rows_out(ft, T_Y)
 
     x_right, x_left, x_far = lax.rem(x + 1, 4), lax.rem(x + 3, 4), lax.rem(x + 2, 4)
@@ -192,32 +189,36 @@
                 asm[12 * s:12 * s + 12, 128 * q:128 * q + 128] = wz_wide[s, 12 * q:12 * q + 12, :]
         wb[h, k, x] = asm[...].astype(BF16)
         own = piece(h, x)
-        copy(own, own, RING + 8 * h, right).start()
-        copy(own, own, RING + 8 * h + 1, left).start()
-        copy(own, own, RING + 8 * h + 4, core).start()
+        at = RING + 10 * h
+        copy(own.at[low], own.at[low], at, right).start()
+        copy(own.at[high], own.at[high], at + 2, left).start()
+        copy(own.at[high], own.at[high], at + 1, right).start()
+        copy(own.at[low], own.at[low], at + 3, left).start()
+        copy(own, own, at + 6, core).start()
         if h == 0:
             rows_on(ft, T_Y)
-    got(sz_buf.at[pl.ds(0, 7)], S_Z)
-    fs[y] = sz_buf[...].reshape(64, 384).astype(BF16)
     rows_out(fs, S_Y)
-    for h in range(2):
-        at, from_left, from_right = RING + 8 * h, piece(h, x_left), piece(h, x_right)
-        got(from_left, at)
-        copy(from_left.at[low], from_left.at[low], at + 2, right).start()
-        got(from_right, at + 1)
-        copy(from_right.at[high], from_right.at[high], at + 3, left).start()
-        copy(from_left, from_left, at + 5, core).start()
-        copy(from_right, from_right, at + 6, core).start()
+    def relay(h):
+        at, from_left, from_right = RING + 10 * h, piece(h, x_left), piece(h, x_right)
+        got(from_left.at[low], at)
+        copy(from_left.at[low], from_left.at[low], at + 4, right).start()
+        got(from_right.at[high], at + 2)
+        copy(from_right.at[high], from_right.at[high], at + 5, left).start()
+        got(from_left.at[high], at + 1)
+        copy(from_left, from_left, at + 7, core).start()
+        got(from_right.at[low], at + 3)
+        copy(from_right, from_right, at + 8, core).start()
 
     def far_piece(h):
         far = piece(h, x_far)
-        got(far.at[low], RING + 8 * h + 2)
-        got(far.at[high], RING + 8 * h + 3)
-        copy(far, far, RING + 8 * h + 7, core).start()
-
+        got(far.at[low], RING + 10 * h + 4)
+        got(far.at[high], RING + 10 * h + 5)
+        copy(far, far, RING + 10 * h + 9, core).start()
+
+    relay(0)
     far_piece(0)
+    relay(1)
     rows_in(ft, T_Y)
-    far_piece(1)
 
     def chunk(q):
         h, kk, c0 = lax.div(q, 4), lax.rem(lax.div(q, 2), 2), pl.multiple_of(lax.rem(q, 2) * 256, 256)
@@ -237,12 +238,18 @@
             csum[pl.ds(2 * q + n, 1), :] = col[:, part]
         return carry
 
+    def teacher_part(h, kk):
+        lax.fori_loop(0, 2, lambda c, carry: teacher_chunk(4 * h + 2 * kk + c, carry), 0)
+
     for h in range(2):
+        if h == 1:
+            far_piece(1)
+        teacher_part(h, k)
+        if h == 1:
+            rows_on(fs, S_Y)
         for n in range(4):
-            got(piece(h, x), RING + 8 * h + 4 + n)
-        lax.fori_loop(4 * h, 4 * h + 4, teacher_chunk, 0)
-        if h == 0:
-            rows_on(fs, S_Y)
+            got(piece(h, x), RING + 10 * h + 6 + n)
+        teacher_part(h, 1 - k)
 
     def columns_start(it):
         c_send[it] = csum[...].astype(BF16)
@@ -436,7 +443,8 @@
     g2a = sum_blocks(g2a_send[a_me], g2a_buf)
     for b in range(8):
         rows, part = crops(a_me, b), slice(8 * b, 8 * b + 8)
-        ua_send[b] = g1a[part] * wide(xb[rows, :], 2) - g2a[part] * wide(rb[rows, :], 2)
+        u = g1a[part] * wide(xb[rows, :], 2) - g2a[part] * wide(rb[rows, :], 2)
+        ua_send[b] = jnp.concatenate([u[:, :128], u[:, 128:]], axis=0).astype(BF16)
     for i in FAR_FIRST:
         copy(ua_send.at[lax.rem(b_me + i, 8)], ua_buf.at[i - 1], U_A, b_peer(i)).start()
 
@@ -447,7 +455,8 @@
     got(ub_buf, U_B)
     u_b = added(ub_send.at[a_me], ub_buf)
     got(ua_buf, U_A)
-    u8 = jnp.concatenate([added(ua_send.at[b_me], ua_buf), u_b], axis=1) * (cot8 / 0.1)
+    u_a = sum_blocks(ua_send[b_me], ua_buf)
+    u8 = jnp.concatenate([u_a[:8], u_a[8:], u_b], axis=1) * (cot8 / 0.1)
     unit8 = own_unit[...]
     along = jnp.sum(unit8 * u8, axis=1, keepdims=True)
     result = ((u8 - unit8 * along) * inv8).astype(BF16)
@@ -469,22 +478,19 @@
     losses = jnp.transpose(out[:, 8:, 128:].reshape(128, 128))
     loss_ref[...] = losses[0:1, :] + losses[64:65, :]
 
-    sent(fz_buf.at[pl.ds(0, 7)], T_Z)
-    sent(sz_buf.at[pl.ds(0, 7)], S_Z)
+    sent(fz_buf.at[pl.ds(0, 7)], F_Z)
     for buf, at in ((ft, T_Y), (fs, S_Y)):
         sent(buf.at[pl.ds(0, 2)], at)
         sent(buf.at[y], at + 1)
         sent(buf.at[y], at + 2)
         sent(buf.at[pl.ds(0, 3)], at + 3)
     for h in range(2):
-        at, own = RING + 8 * h, piece(h, x)
+        at, own = RING + 10 * h, piece(h, x)
         sent(wz_buf.at[h, pl.ds(0, 7)], W_Z + h)
-        sent(own, at)
-        sent(own, at + 1)
-        sent(own.at[low], at + 2)
-        sent(own.at[low], at + 3)
-        for n in range(4):
-            sent(own, at + 4 + n)
+        for n in range(6):
+            sent(own.at[low], at + n)
+        for n in range(6, 10):
+            sent(own, at + n)
     for it in range(3):
         sent(c_buf.at[it], COLS + it)
         _, y_buf, _, z_buf = row_refs(it)
@@ -510,8 +516,7 @@
             v((16, 384), BF16), v((16, 384), BF16), v((12, 8192), BF16), v((1, 128), F32), v((384, 384), BF16),
             v((768, 128), F32), v((2, 8, 48, 128), BF16), v((2, 8, 48, 128), BF16), v((8, 48, 128), F32),
             v((96, 512), F32), v((2, 2, 4, 96, 512), BF16),
-            v((8, 384), F32), v((8, 8, 384), F32), v((8, 64, 384), BF16),
-            v((8, 384), F32), v((8, 8, 384), F32), v((8, 64, 384), BF16),
+            v((48, 128), BF16), v((8, 48, 128), BF16), v((8, 64, 384), BF16), v((8, 64, 384), BF16),
             v((512, 2048), F32), v((512, 2048), F32), v((512, 2048), BF16),
             v((512, 128), F32), v((512, 128), F32), v((512, 128), F32), v((512, 128), F32), v((512, 128), F32),
             v((16, 128), F32), v((16, 128), F32),
@@ -520,7 +525,7 @@
             v((512, 256), F32), v((512, 128), F32),
             v((8, 64, 256), BF16), v((7, 64, 256), BF16), v((8, 64, 128), BF16), v((7, 64, 128), BF16),
             v((8, 64, 256), BF16), v((7, 64, 256), BF16), v((8, 64, 128), BF16), v((7, 64, 128), BF16),
-            v((8, 8, 256), F32), v((7, 8, 256), F32), v((8, 8, 128), F32), v((7, 8, 128), F32),
+            v((8, 16, 128), BF16), v((7, 16, 128), BF16), v((8, 8, 128), F32), v((7, 8, 128), F32),
             v((16, 128), F32), v((16, 128), F32), v((16, 128), F32), v((7, 16, 128), F32), v((16, 128), F32), v((7, 16, 128), F32),
             v((128, 128), F32), v((128, 128), F32), v((8, 384), F32),
             v((16, 256), BF16), v((2, 8, 16, 256), BF16),

time: 93.6 us -> 92.6 us (0.989)
  Pallas kernels: 91.6 us -> 90.6 us
    pallas_call x1, Pallas kernels: 91.6 us -> 90.6 us  [shards(): pl.pallas_call(kernel, out_shape=(v((128, 384), F32), v((1, 128), F32)),...]
where the time goes in v2:
time: 92.6 us; the launch traced here: 92.5 us
  Pallas kernels  90.6 us (98%)
  local copies, waits for them, and re-layouts  1.19 us (1%)
    pallas_call x1, Pallas kernels, shards(): pl.pallas_call(kernel, out_shape=(v((128, 384), F32), v((1, 128), F32)),...  90.6 us

profile of v2, /device:TPU:1, one launch (start us, length us, event | category | flops | bytes accessed | tf_op | source)
XLA Modules:
  0.0 92.5 jit_solution(3677043531807955076)
XLA Ops:
  0.6 90.6 %shard_map.59 = (f32[128,384]{1,0:T(8,128)S(1)}, f32[1,128]{1,0:T(1,128)S(1)}) custom-call(bf16[128,384]{1,0:T(8,128)(2,1)} %t_hbm.1, bf16[128,384]{1,0:T(8,128)(2,1)} %s_hbm.1, bf16[12,8192]{1,0:T(8,128)(2,1)} %w_hbm.1, f32[1,128]{1,0:T(1,128)} %bitcast.3), custom_call_target="tpu_custom_call" | custom-call | flops 2400000000 | bytes 4000000 | tf_op jit(solution)/shard_map/pallas_call | solution.py:510
  91.3 0.5 copy.8
  91.8 0.7 copy.9

commit v3 on v2

--- a/solution.py
+++ b/solution.py
@@ -22,9 +22,10 @@
 RING = 4
 COLS = 24
 ROW_Y, ROW_Z = 27, 30
-G1_A, G1_B, G2_A, G2_B, U_A, U_B, FIN, FIN_CORE = range(33, 41)
-T_Y, S_Y = 41, 45
-COUNT = 49
+G1, G2 = 33, 36
+U_A, U_B, FIN = 39, 40, 41
+T_Y, S_Y = 42, 46
+COUNT = 50
 
 
 def unit_rows(values):
@@ -46,7 +47,7 @@
     fz_send, fz_buf, ft, fs,
     e_ref, l_ref, pb, rowacc, rowacc2, eacc, rb, xb, ivec, cvec,
     c_send, c_buf, ry_send, ry_buf, rz_send, rz_buf,
-    ga, gb, g1a_send, g1a_buf, g1b_send, g1b_buf, g2a_send, g2a_buf, g2b_send, g2b_buf,
+    gs, g1_send, g1_buf, g2_send, g2_buf,
     ua_send, ua_buf, ub_send, ub_buf, csum, vec, lry_send, lry_buf, lrz_send, lrz_buf,
     col_cot, col_x, own_unit,
     fin_send, fin_buf,
@@ -66,6 +67,9 @@
         g = lax.rem(x * 2 + k + i, 8)
         return (z * 4 + lax.div(g, 2), y * 2 + lax.rem(g, 2))
 
+    def y_cross(i):
+        return (dp, lax.rem(y + i, 8) * 2 + 1 - k)
+
     def a_peer(i):
         y_at, z_at = y_peer(i)[1], z_peer(i)[0]
         return (dp + k * (z_at - dp), y_at + k * (pr - y_at))
@@ -98,7 +102,7 @@
     loads = [
         pltpu.make_async_copy(src, dst, lsem.at[n])
         for n, (src, dst) in enumerate((
-            (t_hbm.at[rows16], t_ref), (w_hbm, w_ref), (s_hbm.at[rows16], s_ref), (cot_hbm, cot_ref)
+            (w_hbm, w_ref), (t_hbm.at[rows16], t_ref), (s_hbm.at[rows16], s_ref), (cot_hbm, cot_ref)
         ))
     ]
     for load in loads:
@@ -106,7 +110,7 @@
 
     barrier = pltpu.get_barrier_semaphore()
     for i in range(1, 8):
-        for peer in (z_peer(i), y_peer(i), xk_peer(i)):
+        for peer in (z_peer(i), y_peer(i), xk_peer(i), y_cross(i)):
             pl.semaphore_signal(barrier, inc=1, device_id=peer, device_id_type=MESH)
 
     feature = lax.broadcasted_iota(jnp.int32, (384, 128), 0)
@@ -118,14 +122,6 @@
         perm_ref[:, 128 * n:128 * n + 128] = (place == lane + 128 * n).astype(F32).astype(BF16)
 
     loads[0].wait()
-    loads[2].wait()
-    v = jnp.concatenate([t_ref[...].astype(F32), s_ref[...].astype(F32)], axis=0)
-    v = jnp.dot(unit_rows(v)[0].astype(BF16), perm_ref[...], preferred_element_type=F32)
-    v = [jnp.where(half == 0, v[at:at + 8], v[at + 8:at + 16]) for at in (0, 16)]
-    v = jnp.concatenate([m[:, 128 * n:128 * n + 128] for m in v for n in range(3)], axis=0).astype(BF16)
-    fz_send[...] = v
-    fz_buf[z] = v
-    loads[1].wait()
     for d in range(8):
         for h in range(2):
             for r in range(4):
@@ -137,13 +133,24 @@
             wz_send[h, d] = pack[at:at + 48, :].astype(BF16)
         wz_buf[h, z] = wz_send[h, z]
 
-    pl.semaphore_wait(barrier, 21)
-
+    pl.semaphore_wait(barrier, 28)
+
+    def weights_out(h):
+        for i in FAR_FIRST:
+            copy(wz_send.at[h, lax.rem(z + i, 8)], wz_buf.at[h, z], W_Z + h, z_peer(i)).start()
+
+    weights_out(0)
+    loads[1].wait()
+    loads[2].wait()
+    v = jnp.concatenate([t_ref[...].astype(F32), s_ref[...].astype(F32)], axis=0)
+    v = jnp.dot(unit_rows(v)[0].astype(BF16), perm_ref[...], preferred_element_type=F32)
+    v = [jnp.where(half == 0, v[at:at + 8], v[at + 8:at + 16]) for at in (0, 16)]
+    v = jnp.concatenate([m[:, 128 * n:128 * n + 128] for m in v for n in range(3)], axis=0).astype(BF16)
+    fz_send[...] = v
+    fz_buf[z] = v
     for i in FAR_FIRST:
         copy(fz_send, fz_buf.at[z], F_Z, z_peer(i)).start()
-    for h in range(2):
-        for i in FAR_FIRST:
-            copy(wz_send.at[h, lax.rem(z + i, 8)], wz_buf.at[h, z], W_Z + h, z_peer(i)).start()
+    weights_out(1)
 
     first, second = pl.ds(0, 32), pl.ds(32, 32)
 
@@ -166,13 +173,6 @@
     def rows_in(buf, at):
         got(buf.at[pl.ds(0, 2)], at)
         got(buf.at[pl.ds(0, 3)], at + 3)
-
-    got(fz_buf.at[pl.ds(0, 7)], F_Z)
-    for buf, at in ((ft, 0), (fs, 24)):
-        v = [fz_buf[d, :, :].astype(F32) for d in range(8)]
-        v = [jnp.concatenate([m[at + 8 * n:at + 8 * n + 8] for m in v], axis=0) for n in range(3)]
-        buf[y] = jnp.concatenate(v, axis=1).astype(BF16)
-    rows_out(ft, T_Y)
 
     x_right, x_left, x_far = lax.rem(x + 1, 4), lax.rem(x + 3, 4), lax.rem(x + 2, 4)
     right, left, core = (z * 4 + x_right, pr), (z * 4 + x_left, pr), (dp, y * 2 + 1 - k)
@@ -196,8 +196,16 @@
         copy(own.at[low], own.at[low], at + 3, left).start()
         copy(own, own, at + 6, core).start()
         if h == 0:
+            got(fz_buf.at[pl.ds(0, 7)], F_Z)
+            for buf, at in ((ft, 0), (fs, 24)):
+                v = [fz_buf[d, :, :].astype(F32) for d in range(8)]
+                v = [jnp.concatenate([m[at + 8 * n:at + 8 * n + 8] for m in v], axis=0) for n in range(3)]
+                buf[y] = jnp.concatenate(v, axis=1).astype(BF16)
+            rows_out(ft, T_Y)
+        else:
             rows_on(ft, T_Y)
-    rows_out(fs, S_Y)
+            rows_out(fs, S_Y)
+
     def relay(h):
         at, from_left, from_right = RING + 10 * h, piece(h, x_left), piece(h, x_right)
         got(from_left.at[low], at)
@@ -340,23 +348,21 @@
             total = term if total is None else total + term
         return total
 
-    def gradient_a(dst):
-        ga[...] = product(0, 256)
-        for a in range(8):
-            dst[a] = jnp.concatenate([ga[crops(a, b), :] for b in range(8)], axis=0).astype(BF16)
-
-    def gradient_b(dst):
-        gb[...] = product(256, 384)
-        for b in range(8):
-            dst[b] = jnp.concatenate([gb[crops(a, b), :] for a in range(8)], axis=0).astype(BF16)
-
-    def spread_a(src, dst, sem):
+    def gradient(p, dst):
+        gs[...] = product(128 * p, 128 * p + 128)
+        for i in range(8):
+            at = [crops(i, j) if p < 2 else crops(j, i) for j in range(8)]
+            dst[p, i] = jnp.concatenate([gs[rows, :] for rows in at], axis=0).astype(BF16)
+
+    def spread(p, src, dst, sem):
+        me, peer = (a_me, a_peer) if p < 2 else (b_me, b_peer)
         for i in FAR_FIRST:
-            copy(src.at[lax.rem(a_me + i, 8)], dst.at[i - 1], sem, a_peer(i)).start()
-
-    def spread_b(src, dst, sem):
-        for i in FAR_FIRST:
-            copy(src.at[lax.rem(b_me + i, 8)], dst.at[i - 1], sem, b_peer(i)).start()
+            copy(src.at[p, lax.rem(me + i, 8)], dst.at[p, i - 1], sem + p, peer(i)).start()
+
+    def gathered(p, src, dst, sem):
+        got(dst.at[p], sem + p)
+        own = src[p, a_me if p < 2 else b_me]
+        return fold([own.astype(F32)] + [dst[p, i].astype(F32) for i in range(7)])
 
     columns_start(0)
     lry_send[...] = jnp.zeros_like(lry_send)
@@ -377,12 +383,14 @@
     columns_end(1)
     row_pass()
     rows_start(1)
-    gradient_a(g1a_send)
+    gradient(0, g1_send)
+    gradient(1, g1_send)
     rows_middle(1)
-    spread_a(g1a_send, g1a_buf, G1_A)
-    gradient_b(g1b_send)
+    spread(0, g1_send, g1_buf, G1)
+    spread(1, g1_send, g1_buf, G1)
+    gradient(2, g1_send)
     rows_end(1)
-    spread_b(g1b_send, g1b_buf, G1_B)
+    spread(2, g1_send, g1_buf, G1)
     column_pass()
     columns_start(2)
     s16 = unit_rows(s_ref[...].astype(F32))
@@ -410,11 +418,13 @@
     lax.fori_loop(0, 32, last_pass, 0, unroll=2)
     put(lry_send, 4, lanes(rowacc2))
     rows_start(2)
-    gradient_a(g2a_send)
-    spread_a(g2a_send, g2a_buf, G2_A)
-    gradient_b(g2b_send)
+    gradient(0, g2_send)
+    spread(0, g2_send, g2_buf, G2)
+    gradient(2, g2_send)
+    spread(2, g2_send, g2_buf, G2)
     rows_middle(2)
-    spread_b(g2b_send, g2b_buf, G2_B)
+    gradient(1, g2_send)
+    spread(1, g2_send, g2_buf, G2)
 
     def sum_blocks(own, buf):
         return fold([own.astype(F32)] + [buf[i].astype(F32) for i in range(7)])
@@ -422,29 +432,24 @@
     def wide(block, times):
         return jnp.concatenate([block] * times, axis=1)
 
-    got(g1a_buf, G1_A)
-    got(g1b_buf, G1_B)
-    g1a = sum_blocks(g1a_send[a_me], g1a_buf)
-    g1b = sum_blocks(g1b_send[b_me], g1b_buf)
+    g1 = [gathered(p, g1_send, g1_buf, G1) for p in range(3)]
     total = rows_end(2)
     vec[...] = total
     inv_total = 1.0 / total[8:12, :]
     for j in range(4):
         xb[128 * j:128 * j + 128, :] = turn(inv_total[j:j + 1, :])
     col_x[...] = turn(vec[pl.ds(lax.div(y, 2) + 4, 1), :])
-    got(g2b_buf, G2_B)
-    g2b = sum_blocks(g2b_send[b_me], g2b_buf)
+    g2b = gathered(2, g2_send, g2_buf, G2)
     for a in range(8):
         rows, part = crops(a, b_me), slice(8 * a, 8 * a + 8)
-        ub_send[a] = g1b[part] * xb[rows, :] - g2b[part] * rb[rows, :]
+        ub_send[a] = g1[2][part] * xb[rows, :] - g2b[part] * rb[rows, :]
     for i in FAR_FIRST:
         copy(ub_send.at[lax.rem(a_me + i, 8)], ub_buf.at[i - 1], U_B, a_peer(i)).start()
-    got(g2a_buf, G2_A)
-    g2a = sum_blocks(g2a_send[a_me], g2a_buf)
+    g2a = [gathered(p, g2_send, g2_buf, G2) for p in range(2)]
     for b in range(8):
         rows, part = crops(a_me, b), slice(8 * b, 8 * b + 8)
-        u = g1a[part] * wide(xb[rows, :], 2) - g2a[part] * wide(rb[rows, :], 2)
-        ua_send[b] = jnp.concatenate([u[:, :128], u[:, 128:]], axis=0).astype(BF16)
+        u = [g1[p][part] * xb[rows, :] - g2a[p][part] * rb[rows, :] for p in range(2)]
+        ua_send[b] = jnp.concatenate(u, axis=0).astype(BF16)
     for i in FAR_FIRST:
         copy(ua_send.at[lax.rem(b_me + i, 8)], ua_buf.at[i - 1], U_A, b_peer(i)).start()
 
@@ -466,13 +471,14 @@
     low_rows, high_rows = result[:, :256], jnp.concatenate([result[:, 256:], loss8], axis=1)
     result = jnp.concatenate([low_rows, high_rows], axis=0).astype(BF16)
     fin_send[...] = result
-    fin_buf[k, y] = result
+    slot = k * 8 + y
+    fin_buf[slot] = result
     for i in FAR_FIRST:
-        copy(fin_send, fin_buf.at[k, y], FIN, y_peer(i)).start()
-    got(fin_buf.at[k, pl.ds(0, 7)], FIN)
-    copy(fin_buf.at[k], fin_buf.at[k], FIN_CORE, core).start()
-    got(fin_buf.at[1 - k], FIN_CORE)
-    out = fin_buf[...].reshape(16, 16, 256).astype(F32)
+        copy(fin_send, fin_buf.at[slot], FIN, y_peer(i)).start()
+        copy(fin_send, fin_buf.at[slot], FIN, y_cross(i)).start()
+    copy(fin_send, fin_buf.at[slot], FIN, core).start()
+    got(fin_buf.at[pl.ds(0, 15)], FIN)
+    out = fin_buf[...].astype(F32)
     grad_ref[:, :256] = out[:, :8, :].reshape(128, 256)
     grad_ref[:, 256:] = out[:, 8:, :128].reshape(128, 128)
     losses = jnp.transpose(out[:, 8:, 128:].reshape(128, 128))
@@ -496,9 +502,12 @@
         _, y_buf, _, z_buf = row_refs(it)
         sent(y_buf, ROW_Y + it)
         sent(z_buf, ROW_Z + it)
+    for p in range(3):
+        sent(g1_buf.at[p], G1 + p)
+        sent(g2_buf.at[p], G2 + p)
     for buf, sem in (
-        (g1a_buf, G1_A), (g1b_buf, G1_B), (g2a_buf, G2_A), (g2b_buf, G2_B), (ua_buf, U_A), (ub_buf, U_B),
-        (fin_buf.at[k, pl.ds(0, 7)], FIN), (fin_buf.at[k], FIN_CORE),
+        (ua_buf, U_A), (ub_buf, U_B),
+        (fin_buf.at[pl.ds(0, 15)], FIN),
     ):
         sent(buf, sem)
 
@@ -522,13 +531,12 @@
             v((16, 128), F32), v((16, 128), F32),
             v((3, 16, 128), BF16), v((3, 7, 16, 128), BF16),
             v((2, 4, 128), F32), v((2, 7, 4, 128), F32), v((2, 4, 128), F32), v((2, 7, 4, 128), F32),
-            v((512, 256), F32), v((512, 128), F32),
-            v((8, 64, 256), BF16), v((7, 64, 256), BF16), v((8, 64, 128), BF16), v((7, 64, 128), BF16),
-            v((8, 64, 256), BF16), v((7, 64, 256), BF16), v((8, 64, 128), BF16), v((7, 64, 128), BF16),
+            v((512, 128), F32),
+            v((3, 8, 64, 128), BF16), v((3, 7, 64, 128), BF16), v((3, 8, 64, 128), BF16), v((3, 7, 64, 128), BF16),
             v((8, 16, 128), BF16), v((7, 16, 128), BF16), v((8, 8, 128), F32), v((7, 8, 128), F32),
             v((16, 128), F32), v((16, 128), F32), v((16, 128), F32), v((7, 16, 128), F32), v((16, 128), F32), v((7, 16, 128), F32),
             v((128, 128), F32), v((128, 128), F32), v((8, 384), F32),
-            v((16, 256), BF16), v((2, 8, 16, 256), BF16),
+            v((16, 256), BF16), v((16, 16, 256), BF16),
             pltpu.SemaphoreType.DMA((4,)), pltpu.SemaphoreType.DMA((COUNT,)), pltpu.SemaphoreType.DMA((COUNT,)),
         ],
         compiler_params=pltpu.CompilerParams(

time: 92.6 us -> 92.3 us (level)
  no operation moved by 1% of the time
where the time goes in v3:
time: 92.3 us; the launch traced here: 92.2 us
  Pallas kernels  90.4 us (98%)
  local copies, waits for them, and re-layouts  1.19 us (1%)
    pallas_call x1, Pallas kernels, shards(): pl.pallas_call(kernel, out_shape=(v((128, 384), F32), v((1, 128), F32)),...  90.4 us

profile of v3, /device:TPU:1, one launch (start us, length us, event | category | flops | bytes accessed | tf_op | source)
XLA Modules:
  0.0 92.2 jit_solution(1986627704563926117)
XLA Ops:
  0.6 90.4 %shard_map.59 = (f32[128,384]{1,0:T(8,128)S(1)}, f32[1,128]{1,0:T(1,128)S(1)}) custom-call(bf16[128,384]{1,0:T(8,128)(2,1)} %t_hbm.1, bf16[128,384]{1,0:T(8,128)(2,1)} %s_hbm.1, bf16[12,8192]{1,0:T(8,128)(2,1)} %w_hbm.1, f32[1,128]{1,0:T(1,128)} %bitcast.3), custom_call_target="tpu_custom_call" | custom-call | flops 2400000000 | bytes 4000000 | tf_op jit(solution)/shard_map/pallas_call | solution.py:519
  91.0 0.5 copy.8
  91.5 0.7 copy.9

commit v4 on v3

--- a/solution.py
+++ b/solution.py
@@ -364,35 +364,39 @@
         own = src[p, a_me if p < 2 else b_me]
         return fold([own.astype(F32)] + [dst[p, i].astype(F32) for i in range(7)])
 
+    def students(first, last):
+        lax.fori_loop(first, last, student_chunk, 0)
+
     columns_start(0)
     lry_send[...] = jnp.zeros_like(lry_send)
     eacc[...] = jnp.zeros_like(eacc)
-    loads[3].wait()
-    col_cot[...] = turn(cot_ref[...])
+    rows_in(fs, S_Y)
+    students(0, 2)
     columns_end(0)
     row_pass()
     rows_start(0)
-    rows_in(fs, S_Y)
-    lax.fori_loop(0, 2, student_chunk, 0)
+    students(2, 4)
     rows_middle(0)
-    lax.fori_loop(2, 5, student_chunk, 0)
+    students(4, 6)
     rows_end(0)
     column_pass()
     columns_start(1)
-    lax.fori_loop(5, 8, student_chunk, 0)
+    students(6, 8)
     columns_end(1)
     row_pass()
     rows_start(1)
     gradient(0, g1_send)
-    gradient(1, g1_send)
     rows_middle(1)
     spread(0, g1_send, g1_buf, G1)
+    gradient(1, g1_send)
+    rows_end(1)
+    column_pass()
+    columns_start(2)
     spread(1, g1_send, g1_buf, G1)
     gradient(2, g1_send)
-    rows_end(1)
     spread(2, g1_send, g1_buf, G1)
-    column_pass()
-    columns_start(2)
+    loads[3].wait()
+    col_cot[...] = turn(cot_ref[...])
     s16 = unit_rows(s_ref[...].astype(F32))
     s8, inv8 = (jnp.where(half == 0, v[0:8], v[8:16]) for v in s16)
     put(lry_send, 8, lanes(eacc))

time: 92.3 us -> 92.3 us (level)
  no operation moved by 1% of the time
where the time goes in v4:
time: 92.3 us; the launch traced here: 92.2 us
  Pallas kernels  90.3 us (98%)
  local copies, waits for them, and re-layouts  1.19 us (1%)
    pallas_call x1, Pallas kernels, shards(): pl.pallas_call(kernel, out_shape=(v((128, 384), F32), v((1, 128), F32)),...  90.3 us

profile of v4, /device:TPU:1, one launch (start us, length us, event | category | flops | bytes accessed | tf_op | source)
XLA Modules:
  0.0 92.2 jit_solution(10452908545783374366)
XLA Ops:
  0.6 90.3 %shard_map.59 = (f32[128,384]{1,0:T(8,128)S(1)}, f32[1,128]{1,0:T(1,128)S(1)}) custom-call(bf16[128,384]{1,0:T(8,128)(2,1)} %t_hbm.1, bf16[128,384]{1,0:T(8,128)(2,1)} %s_hbm.1, bf16[12,8192]{1,0:T(8,128)(2,1)} %w_hbm.1, f32[1,128]{1,0:T(1,128)} %bitcast.3), custom_call_target="tpu_custom_call" | custom-call | flops 2400000000 | bytes 4000000 | tf_op jit(solution)/shard_map/pallas_call | solution.py:523
  91.0 0.5 copy.8
  91.5 0.7 copy.9

commit v5 on v4

--- a/solution.py
+++ b/solution.py
@@ -21,7 +21,7 @@
 F_Z, W_Z = 0, 1
 RING = 4
 COLS = 24
-ROW_Y, ROW_Z = 27, 30
+ROWS, LAST_Y, LAST_Z = 27, 29, 30
 G1, G2 = 33, 36
 U_A, U_B, FIN = 39, 40, 41
 T_Y, S_Y = 42, 46
@@ -46,7 +46,7 @@
     pack, wz_send, wz_buf, wz_wide, asm, wb,
     fz_send, fz_buf, ft, fs,
     e_ref, l_ref, pb, rowacc, rowacc2, eacc, rb, xb, ivec, cvec,
-    c_send, c_buf, ry_send, ry_buf, rz_send, rz_buf,
+    c_send, c_buf, r_send, r_buf,
     gs, g1_send, g1_buf, g2_send, g2_buf,
     ua_send, ua_buf, ub_send, ub_buf, csum, vec, lry_send, lry_buf, lrz_send, lrz_buf,
     col_cot, col_x, own_unit,
@@ -66,6 +66,11 @@
     def xk_peer(i):
         g = lax.rem(x * 2 + k + i, 8)
         return (z * 4 + lax.div(g, 2), y * 2 + lax.rem(g, 2))
+
+    def plane_peer(i, j):
+        return (z_peer(i)[0], y_peer(j)[1])
+
+    plane = [(i, j) for i in FAR_FIRST + (0,) for j in FAR_FIRST + (0,)][:-1]
 
     def y_cross(i):
         return (dp, lax.rem(y + i, 8) * 2 + 1 - k)
@@ -110,8 +115,10 @@
 
     barrier = pltpu.get_barrier_semaphore()
     for i in range(1, 8):
-        for peer in (z_peer(i), y_peer(i), xk_peer(i), y_cross(i)):
+        for peer in (xk_peer(i), y_cross(i)):
             pl.semaphore_signal(barrier, inc=1, device_id=peer, device_id_type=MESH)
+    for i, j in plane:
+        pl.semaphore_signal(barrier, inc=1, device_id=plane_peer(i, j), device_id_type=MESH)
 
     feature = lax.broadcasted_iota(jnp.int32, (384, 128), 0)
     fz = lax.shift_right_logical(feature * 1366, 16)
@@ -133,7 +140,7 @@
             wz_send[h, d] = pack[at:at + 48, :].astype(BF16)
         wz_buf[h, z] = wz_send[h, z]
 
-    pl.semaphore_wait(barrier, 28)
+    pl.semaphore_wait(barrier, 77)
 
     def weights_out(h):
         for i in FAR_FIRST:
@@ -285,37 +292,47 @@
         for j in range(4):
             dst[at + j:at + j + 1, :] = sums[j]
 
-    def row_refs(it):
-        if it == 2:
-            return lry_send, lry_buf, lrz_send, lrz_buf
-        return ry_send.at[it], ry_buf.at[it], rz_send.at[it], rz_buf.at[it]
+    def tree(terms):
+        while len(terms) > 1:
+            pairs = [a + b for a, b in zip(terms[::2], terms[1::2])]
+            terms = pairs + terms[2 * len(pairs):]
+        return terms[0]
 
     def added(own, buf):
-        return fold([own[...]] + [buf[i] for i in range(7)])
-
-    def rows_start(it):
-        y_send, y_buf, _, _ = row_refs(it)
-        put(y_send, 0, lanes(rowacc))
-        for i in FAR_FIRST:
-            copy(y_send, y_buf.at[i - 1], ROW_Y + it, y_peer(i)).start()
-
-    def rows_middle(it):
-        y_send, y_buf, z_send, z_buf = row_refs(it)
-        got(y_buf, ROW_Y + it)
-        z_send[...] = added(y_send, y_buf)
-        for i in FAR_FIRST:
-            copy(z_send, z_buf.at[i - 1], ROW_Z + it, z_peer(i)).start()
+        return tree([own[...]] + [buf[i] for i in range(buf.shape[0])])
 
     def turn(row):
         return jnp.transpose(jnp.broadcast_to(row, (128, 128)))
 
-    def rows_end(it):
-        _, _, z_send, z_buf = row_refs(it)
-        got(z_buf, ROW_Z + it)
-        total = added(z_send, z_buf)
+    def set_row_scale(total):
         r = 1.0 / total[0:4, :]
         for j in range(4):
             rb[128 * j:128 * j + 128, :] = turn(r[j:j + 1, :])
+
+    def rows_start(it):
+        put(r_send.at[it], 0, lanes(rowacc))
+        for n, (i, j) in enumerate(plane):
+            copy(r_send.at[it], r_buf.at[it, n], ROWS + it, plane_peer(i, j)).start()
+
+    def rows_end(it):
+        got(r_buf.at[it], ROWS + it)
+        set_row_scale(added(r_send.at[it], r_buf.at[it]))
+
+    def last_rows_start():
+        put(lry_send, 0, lanes(rowacc))
+        for i in FAR_FIRST:
+            copy(lry_send, lry_buf.at[i - 1], LAST_Y, y_peer(i)).start()
+
+    def last_rows_middle():
+        got(lry_buf, LAST_Y)
+        lrz_send[...] = added(lry_send, lry_buf)
+        for i in FAR_FIRST:
+            copy(lrz_send, lrz_buf.at[i - 1], LAST_Z, z_peer(i)).start()
+
+    def last_rows_end():
+        got(lrz_buf, LAST_Z)
+        total = added(lrz_send, lrz_buf)
+        set_row_scale(total)
         return total
 
     def column_pass():
@@ -375,21 +392,18 @@
     columns_end(0)
     row_pass()
     rows_start(0)
-    students(2, 4)
-    rows_middle(0)
-    students(4, 6)
+    students(2, 5)
     rows_end(0)
     column_pass()
     columns_start(1)
-    students(6, 8)
+    students(5, 8)
     columns_end(1)
     row_pass()
     rows_start(1)
     gradient(0, g1_send)
-    rows_middle(1)
-    spread(0, g1_send, g1_buf, G1)
     gradient(1, g1_send)
     rows_end(1)
+    spread(0, g1_send, g1_buf, G1)
     column_pass()
     columns_start(2)
     spread(1, g1_send, g1_buf, G1)
@@ -421,12 +435,12 @@
 
     lax.fori_loop(0, 32, last_pass, 0, unroll=2)
     put(lry_send, 4, lanes(rowacc2))
-    rows_start(2)
+    last_rows_start()
     gradient(0, g2_send)
     spread(0, g2_send, g2_buf, G2)
     gradient(2, g2_send)
     spread(2, g2_send, g2_buf, G2)
-    rows_middle(2)
+    last_rows_middle()
     gradient(1, g2_send)
     spread(1, g2_send, g2_buf, G2)
 
@@ -437,7 +451,7 @@
         return jnp.concatenate([block] * times, axis=1)
 
     g1 = [gathered(p, g1_send, g1_buf, G1) for p in range(3)]
-    total = rows_end(2)
+    total = last_rows_end()
     vec[...] = total
     inv_total = 1.0 / total[8:12, :]
     for j in range(4):
@@ -503,9 +517,10 @@
             sent(own, at + n)
     for it in range(3):
         sent(c_buf.at[it], COLS + it)
-        _, y_buf, _, z_buf = row_refs(it)
-        sent(y_buf, ROW_Y + it)
-        sent(z_buf, ROW_Z + it)
+    for it in range(2):
+        sent(r_buf.at[it], ROWS + it)
+    sent(lry_buf, LAST_Y)
+    sent(lrz_buf, LAST_Z)
     for p in range(3):
         sent(g1_buf.at[p], G1 + p)
         sent(g2_buf.at[p], G2 + p)
@@ -534,7 +549,7 @@
             v((512, 128), F32), v((512, 128), F32), v((512, 128), F32), v((512, 128), F32), v((512, 128), F32),
             v((16, 128), F32), v((16, 128), F32),
             v((3, 16, 128), BF16), v((3, 7, 16, 128), BF16),
-            v((2, 4, 128), F32), v((2, 7, 4, 128), F32), v((2, 4, 128), F32), v((2, 7, 4, 128), F32),
+            v((2, 4, 128), F32), v((2, 63, 4, 128), F32),
             v((512, 128), F32),
             v((3, 8, 64, 128), BF16), v((3, 7, 64, 128), BF16), v((3, 8, 64, 128), BF16), v((3, 7, 64, 128), BF16),
             v((8, 16, 128), BF16), v((7, 16, 128), BF16), v((8, 8, 128), F32), v((7, 8, 128), F32),

time: 92.3 us -> 91.9 us (level)
  no operation moved by 1% of the time
where the time goes in v5:
time: 91.9 us; the launch traced here: 91.8 us
  Pallas kernels  90 us (98%)
  local copies, waits for them, and re-layouts  1.19 us (1%)
    pallas_call x1, Pallas kernels, shards(): pl.pallas_call(kernel, out_shape=(v((128, 384), F32), v((1, 128), F32)),...  90 us

profile of v5, /device:TPU:1, one launch (start us, length us, event | category | flops | bytes accessed | tf_op | source)
XLA Modules:
  0.0 91.8 jit_solution(16680722222029346824)
XLA Ops:
  0.6 90.0 %shard_map.59 = (f32[128,384]{1,0:T(8,128)S(1)}, f32[1,128]{1,0:T(1,128)S(1)}) custom-call(bf16[128,384]{1,0:T(8,128)(2,1)} %t_hbm.1, bf16[128,384]{1,0:T(8,128)(2,1)} %s_hbm.1, bf16[12,8192]{1,0:T(8,128)(2,1)} %w_hbm.1, f32[1,128]{1,0:T(1,128)} %bitcast.3), custom_call_target="tpu_custom_call" | custom-call | flops 2400000000 | bytes 4000000 | tf_op jit(solution)/shard_map/pallas_call | solution.py:538
  90.6 0.5 copy.8
  91.1 0.7 copy.9

commit v6 on v5

--- a/solution.py
+++ b/solution.py
@@ -440,12 +440,9 @@
     spread(0, g2_send, g2_buf, G2)
     gradient(2, g2_send)
     spread(2, g2_send, g2_buf, G2)
-    last_rows_middle()
     gradient(1, g2_send)
     spread(1, g2_send, g2_buf, G2)
-
-    def sum_blocks(own, buf):
-        return fold([own.astype(F32)] + [buf[i].astype(F32) for i in range(7)])
+    last_rows_middle()
 
     def wide(block, times):
         return jnp.concatenate([block] * times, axis=1)
@@ -467,7 +464,7 @@
     for b in range(8):
         rows, part = crops(a_me, b), slice(8 * b, 8 * b + 8)
         u = [g1[p][part] * xb[rows, :] - g2a[p][part] * rb[rows, :] for p in range(2)]
-        ua_send[b] = jnp.concatenate(u, axis=0).astype(BF16)
+        ua_send[b] = jnp.concatenate(u, axis=0)
     for i in FAR_FIRST:
         copy(ua_send.at[lax.rem(b_me + i, 8)], ua_buf.at[i - 1], U_A, b_peer(i)).start()
 
@@ -478,7 +475,7 @@
     got(ub_buf, U_B)
     u_b = added(ub_send.at[a_me], ub_buf)
     got(ua_buf, U_A)
-    u_a = sum_blocks(ua_send[b_me], ua_buf)
+    u_a = added(ua_send.at[b_me], ua_buf)
     u8 = jnp.concatenate([u_a[:8], u_a[8:], u_b], axis=1) * (cot8 / 0.1)
     unit8 = own_unit[...]
     along = jnp.sum(unit8 * u8, axis=1, keepdims=True)
@@ -552,7 +549,7 @@
             v((2, 4, 128), F32), v((2, 63, 4, 128), F32),
             v((512, 128), F32),
             v((3, 8, 64, 128), BF16), v((3, 7, 64, 128), BF16), v((3, 8, 64, 128), BF16), v((3, 7, 64, 128), BF16),
-            v((8, 16, 128), BF16), v((7, 16, 128), BF16), v((8, 8, 128), F32), v((7, 8, 128), F32),
+            v((8, 16, 128), F32), v((7, 16, 128), F32), v((8, 8, 128), F32), v((7, 8, 128), F32),
             v((16, 128), F32), v((16, 128), F32), v((16, 128), F32), v((7, 16, 128), F32), v((16, 128), F32), v((7, 16, 128), F32),
             v((128, 128), F32), v((128, 128), F32), v((8, 384), F32),
             v((16, 256), BF16), v((16, 16, 256), BF16),

time: 91.9 us -> 91.1 us (level)
  no operation moved by 1% of the time
where the time goes in v6:
time: 91.1 us; the launch traced here: 90.9 us
  Pallas kernels  89.1 us (98%)
  local copies, waits for them, and re-layouts  1.19 us (1%)
    pallas_call x1, Pallas kernels, shards(): pl.pallas_call(kernel, out_shape=(v((128, 384), F32), v((1, 128), F32)),...  89.1 us

profile of v6, /device:TPU:1, one launch (start us, length us, event | category | flops | bytes accessed | tf_op | source)
XLA Modules:
  0.0 90.9 jit_solution(1091676410923880264)
XLA Ops:
  0.6 89.1 %shard_map.59 = (f32[128,384]{1,0:T(8,128)S(1)}, f32[1,128]{1,0:T(1,128)S(1)}) custom-call(bf16[128,384]{1,0:T(8,128)(2,1)} %t_hbm.1, bf16[128,384]{1,0:T(8,128)(2,1)} %s_hbm.1, bf16[12,8192]{1,0:T(8,128)(2,1)} %w_hbm.1, f32[1,128]{1,0:T(1,128)} %bitcast.3), custom_call_target="tpu_custom_call" | custom-call | flops 2400000000 | bytes 4000000 | tf_op jit(solution)/shard_map/pallas_call | solution.py:535
  89.7 0.5 copy.8
  90.3 0.7 copy.9

commit v7 on v6

--- a/solution.py
+++ b/solution.py
@@ -25,7 +25,8 @@
 G1, G2 = 33, 36
 U_A, U_B, FIN = 39, 40, 41
 T_Y, S_Y = 42, 46
-COUNT = 50
+EXP_Y, EXP_Z = 50, 51
+COUNT = 52
 
 
 def unit_rows(values):
@@ -49,6 +50,7 @@
     c_send, c_buf, r_send, r_buf,
     gs, g1_send, g1_buf, g2_send, g2_buf,
     ua_send, ua_buf, ub_send, ub_buf, csum, vec, lry_send, lry_buf, lrz_send, lrz_buf,
+    ey_send, ey_buf, ez_send, ez_buf,
     col_cot, col_x, own_unit,
     fin_send, fin_buf,
     lsem, ssem, rsem,
@@ -385,7 +387,6 @@
         lax.fori_loop(first, last, student_chunk, 0)
 
     columns_start(0)
-    lry_send[...] = jnp.zeros_like(lry_send)
     eacc[...] = jnp.zeros_like(eacc)
     rows_in(fs, S_Y)
     students(0, 2)
@@ -397,11 +398,18 @@
     column_pass()
     columns_start(1)
     students(5, 8)
+    put(ey_send, 0, lanes(eacc))
+    for i in FAR_FIRST:
+        copy(ey_send, ey_buf.at[i - 1], EXP_Y, y_peer(i)).start()
     columns_end(1)
     row_pass()
     rows_start(1)
     gradient(0, g1_send)
     gradient(1, g1_send)
+    got(ey_buf, EXP_Y)
+    ez_send[...] = added(ey_send, ey_buf)
+    for i in FAR_FIRST:
+        copy(ez_send, ez_buf.at[i - 1], EXP_Z, z_peer(i)).start()
     rows_end(1)
     spread(0, g1_send, g1_buf, G1)
     column_pass()
@@ -413,7 +421,10 @@
     col_cot[...] = turn(cot_ref[...])
     s16 = unit_rows(s_ref[...].astype(F32))
     s8, inv8 = (jnp.where(half == 0, v[0:8], v[8:16]) for v in s16)
-    put(lry_send, 8, lanes(eacc))
+    got(ez_buf, EXP_Z)
+    inv_total = 1.0 / added(ez_send, ez_buf)
+    for j in range(4):
+        xb[128 * j:128 * j + 128, :] = turn(inv_total[j:j + 1, :])
     own_unit[...] = jnp.dot(s8, perm_ref[...].astype(F32), precision=HIGHEST, preferred_element_type=F32)
     columns_end(2)
 
@@ -450,9 +461,6 @@
     g1 = [gathered(p, g1_send, g1_buf, G1) for p in range(3)]
     total = last_rows_end()
     vec[...] = total
-    inv_total = 1.0 / total[8:12, :]
-    for j in range(4):
-        xb[128 * j:128 * j + 128, :] = turn(inv_total[j:j + 1, :])
     col_x[...] = turn(vec[pl.ds(lax.div(y, 2) + 4, 1), :])
     g2b = gathered(2, g2_send, g2_buf, G2)
     for a in range(8):
@@ -516,6 +524,8 @@
         sent(c_buf.at[it], COLS + it)
     for it in range(2):
         sent(r_buf.at[it], ROWS + it)
+    sent(ey_buf, EXP_Y)
+    sent(ez_buf, EXP_Z)
     sent(lry_buf, LAST_Y)
     sent(lrz_buf, LAST_Z)
     for p in range(3):
@@ -550,7 +560,8 @@
             v((512, 128), F32),
             v((3, 8, 64, 128), BF16), v((3, 7, 64, 128), BF16), v((3, 8, 64, 128), BF16), v((3, 7, 64, 128), BF16),
             v((8, 16, 128), F32), v((7, 16, 128), F32), v((8, 8, 128), F32), v((7, 8, 128), F32),
-            v((16, 128), F32), v((16, 128), F32), v((16, 128), F32), v((7, 16, 128), F32), v((16, 128), F32), v((7, 16, 128), F32),
+            v((16, 128), F32), v((8, 128), F32), v((8, 128), F32), v((7, 8, 128), F32), v((8, 128), F32), v((7, 8, 128), F32),
+            v((4, 128), F32), v((7, 4, 128), F32), v((4, 128), F32), v((7, 4, 128), F32),
             v((128, 128), F32), v((128, 128), F32), v((8, 384), F32),
             v((16, 256), BF16), v((16, 16, 256), BF16),
             pltpu.SemaphoreType.DMA((4,)), pltpu.SemaphoreType.DMA((COUNT,)), pltpu.SemaphoreType.DMA((COUNT,)),

time: 91.1 us -> 91.3 us (level)
  no operation moved by 1% of the time
where the time goes in v7:
time: 91.3 us; the launch traced here: 91.2 us
  Pallas kernels  89.3 us (98%)
  local copies, waits for them, and re-layouts  1.19 us (1%)
    pallas_call x1, Pallas kernels, shards(): pl.pallas_call(kernel, out_shape=(v((128, 384), F32), v((1, 128), F32)),...  89.3 us

profile of v7, /device:TPU:1, one launch (start us, length us, event | category | flops | bytes accessed | tf_op | source)
XLA Modules:
  0.0 91.2 jit_solution(61394860427871972)
XLA Ops:
  0.6 89.3 %shard_map.59 = (f32[128,384]{1,0:T(8,128)S(1)}, f32[1,128]{1,0:T(1,128)S(1)}) custom-call(bf16[128,384]{1,0:T(8,128)(2,1)} %t_hbm.1, bf16[128,384]{1,0:T(8,128)(2,1)} %s_hbm.1, bf16[12,8192]{1,0:T(8,128)(2,1)} %w_hbm.1, f32[1,128]{1,0:T(1,128)} %bitcast.3), custom_call_target="tpu_custom_call" | custom-call | flops 2400000000 | bytes 4000000 | tf_op jit(solution)/shard_map/pallas_call | solution.py:545
  90.0 0.5 copy.8
  90.5 0.7 copy.9
